TPU v7x, 32 devices: a whole 2x2x4 slice. The times are simulated.
32 devices in a mesh: tm: 4 (over y, core), panel: 8 (over z, x).
Axes of the slice: x: 2, y: 2, z: 4, core: 2. Of those that a mesh axis runs over, the one named last changes fastest.
Arguments:
- pressure: float32 [4096, 16384], P('tm', 'panel'), may hold values from -6 to 6
- freq_bins: int32 [64], replicated, may hold values from 1 to 2047
- stencil_ids: int32 [4096, 16], P('panel'), may hold values from 0 to 2047
- spline_weights: float32 [4096, 16], P('panel'), may hold values from -2 to 2
- mode_forces: float32 [32, 4096], P(None, 'panel'), may hold values from -0.09375 to 0.09375
- mode_washes: float32 [32, 4096], P(None, 'panel'), may hold values from -6 to 6
Outputs:
- grams: float32 [2, 64, 32, 32], replicated
Inputs may be any that keep to these rules, and one draw needn't show every extreme that they name: `freq_bins`: frequency bins of the excitation lines, possibly repeated. `stencil_ids`: indices within the point group of the panel, group p // 512.
All inputs are finite; a program needn't handle non-finite values.
Results may differ from a plain program's by a relative error of at most 0.000073.
Values sent between devices are 32-bit elements; how exact they have to be, the bound alone decides.
A program may use at most 64 MiB of HBM per device.

v0:
```python
import math
import jax
import jax.numpy as jnp
from jax import lax
from jax.sharding import PartitionSpec as P


def dft_table(freq_bins, first, length, total):
    times = first + jnp.arange(length, dtype=jnp.int32)
    phase = freq_bins[:, None] * times[None, :] % total
    angle = 2.0 * math.pi / total * phase.astype(jnp.float32)
    scale_value = 1.0 / math.sqrt(total)
    return jnp.concatenate([jnp.cos(angle), -jnp.sin(angle)], axis=0) * scale_value


def modal_matrices(panel_spectra, forces_own, washes_own):
    weighted = panel_spectra[:, None, :] * forces_own[None, :, :]
    return lax.dot_general(
        weighted,
        washes_own,
        (((2,), (1,)), ((), ())),
        precision=lax.Precision.HIGHEST,
        preferred_element_type=jnp.float32,
    )


def spline_basis(point_ids, stencil_ids, spline_weights):

    def add_column(column, basis):
        ids_column = lax.dynamic_slice_in_dim(stencil_ids, column, 1, 1)[:, 0]
        weight_column = lax.dynamic_slice_in_dim(spline_weights, column, 1, 1)[:, 0]
        hits = point_ids[:, None] == ids_column[None, :]
        return basis + jnp.where(hits, weight_column[None, :], jnp.float32(0.0))

    start_basis = jnp.zeros((point_ids.shape[0], stencil_ids.shape[0]), jnp.float32)
    return lax.fori_loop(0, stencil_ids.shape[1], add_column, start_basis)


def body(pressure, freq_bins, stencil_ids, spline_weights, mode_forces, mode_washes):
    tm_count = lax.axis_size("tm")
    steps_local = pressure.shape[0]
    steps_total = steps_local * tm_count
    points_local = pressure.shape[1] // tm_count
    point_ids = lax.axis_index("tm") * points_local + jnp.arange(points_local, dtype=jnp.int32)
    local_table = dft_table(freq_bins, lax.axis_index("tm") * steps_local, steps_local, steps_total)
    spectra_rows = lax.psum_scatter(
        lax.dot_general(
            pressure,
            local_table,
            (((0,), (1,)), ((), ())),
            precision=lax.Precision.HIGHEST,
            preferred_element_type=jnp.float32,
        ),
        "tm",
        scatter_dimension=0,
        tiled=True,
    )
    basis = spline_basis(point_ids, stencil_ids, spline_weights)
    partial_spectra = lax.dot_general(
        spectra_rows,
        basis,
        (((0,), (0,)), ((), ())),
        precision=lax.Precision.HIGHEST,
        preferred_element_type=jnp.float32,
    )
    owned = lax.psum_scatter(partial_spectra, "tm", scatter_dimension=1, tiled=True)
    owned_width = owned.shape[1]
    begin = lax.axis_index("tm") * owned_width
    forces_own = lax.dynamic_slice_in_dim(mode_forces, begin, owned_width, 1)
    washes_own = lax.dynamic_slice_in_dim(mode_washes, begin, owned_width, 1)
    local_grams = modal_matrices(owned, forces_own, washes_own)
    summed = lax.psum(local_grams, ("tm", "panel"))
    modes = mode_forces.shape[0]
    return summed.reshape(2, -1, modes, modes)


def solution(mesh):
    placed = (
        P("tm", "panel"),
        P(),
        P("panel", None),
        P("panel", None),
        P(None, "panel"),
        P(None, "panel"),
    )
    return jax.shard_map(body, mesh=mesh, in_specs=placed, out_specs=P(), check_vma=False)
```

profile of v0, /device:TPU:0, one launch (start us, length us, event | category | flops | bytes accessed | tf_op | source)
XLA Modules:
  0.0 212.8 jit_solution(4548003467514517349)
XLA Ops:
  6.5 1.8 fusion.12
  8.3 7.8 %convolution_bitcast_fusion = f32[2048,128]{0,1:T(8,128)} fusion(f32[1024,2048]{1,0:T(8,128)} %param.8, f32[64,1024]{1,0:T(8,128)S(1)} %get-tuple-element.132, f32[64,1024]{1,0:T(8,128)S(1)} %get-tuple-element.131), kind=kOutput, calls=%fused_computation.5 | convolution fusion | flops 3221487616 | bytes 9961472 | tf_op jit(solution)/shard_map/dot_general | solution.py:47
  16.2 0.0 reduce-scatter.3.cloned.1.call-update
  16.2 0.0 reduce-scatter.5.cloned.1.call-start
  16.3 27.4 %while.14 = (s32[]{:T(128)}, f32[512,512]{1,0:T(8,128)S(1)}, s32[512,16]{0,1:T(8,128)}, f32[512,16]{0,1:T(8,128)}, s32[]{:T(128)}, /*index=5*/s32[]{:T(128)}, s32[]{:T(128)}) while((s32[]{:T(128)}, f32[512,512]{1,0:T(8,128)S(1)}, s32[512,16]{0,1:T(8,128)}, f32[512,16]{0,1:T(8,128)}, s32[]{:T(128)}, /*index=5*/s32[]{:T(128)}, ...), condition=%wide.region_2.3_spmd.clone, body=%wide.region_1.2_spmd.clone.sunk | while | flops 1049091 | bytes 2113643 | solution.py:36
  16.3 0.7 constant_dynamic-slice_fusion.5
  17.0 0.7 constant_dynamic-slice_fusion.6
  17.7 0.2 select_add_fusion.2
  18.0 0.7 constant_dynamic-slice_fusion.5
  18.7 0.7 constant_dynamic-slice_fusion.6
  19.4 0.2 select_add_fusion.2
  19.7 0.7 constant_dynamic-slice_fusion.5
  20.4 0.7 constant_dynamic-slice_fusion.6
  21.2 0.2 select_add_fusion.2
  21.4 0.7 constant_dynamic-slice_fusion.5
  22.1 0.7 constant_dynamic-slice_fusion.6
  22.9 0.2 select_add_fusion.2
  23.1 0.7 constant_dynamic-slice_fusion.5
  23.8 0.7 constant_dynamic-slice_fusion.6
  24.6 0.2 select_add_fusion.2
  24.8 0.7 constant_dynamic-slice_fusion.5
  25.6 0.7 constant_dynamic-slice_fusion.6
  26.3 0.2 select_add_fusion.2
  26.5 0.7 constant_dynamic-slice_fusion.5
  27.3 0.7 constant_dynamic-slice_fusion.6
  28.0 0.2 select_add_fusion.2
  28.3 0.7 constant_dynamic-slice_fusion.5
  29.0 0.7 constant_dynamic-slice_fusion.6
  29.7 0.2 select_add_fusion.2
  30.0 0.7 constant_dynamic-slice_fusion.5
  30.7 0.7 constant_dynamic-slice_fusion.6
  31.4 0.2 select_add_fusion.2
  31.7 0.7 constant_dynamic-slice_fusion.5
  32.4 0.7 constant_dynamic-slice_fusion.6
  33.1 0.2 select_add_fusion.2
  33.4 0.7 constant_dynamic-slice_fusion.5
  34.1 0.7 constant_dynamic-slice_fusion.6
  34.8 0.2 select_add_fusion.2
  35.1 0.7 constant_dynamic-slice_fusion.5
  35.8 0.7 constant_dynamic-slice_fusion.6
  36.6 0.2 select_add_fusion.2
  36.8 0.7 constant_dynamic-slice_fusion.5
  37.5 0.7 constant_dynamic-slice_fusion.6
  38.3 0.2 select_add_fusion.2
  38.5 0.7 constant_dynamic-slice_fusion.5
  39.2 0.7 constant_dynamic-slice_fusion.6
  40.0 0.2 select_add_fusion.2
  40.2 0.7 constant_dynamic-slice_fusion.5
  41.0 0.7 constant_dynamic-slice_fusion.6
  41.7 0.2 select_add_fusion.2
  41.9 0.7 constant_dynamic-slice_fusion.5
  42.7 0.7 constant_dynamic-slice_fusion.6
  43.4 0.2 select_add_fusion.2
  43.6 0.3 reduce-scatter.3.cloned.1.call-done
  43.9 2.4 %fusion.18 = f32[128,512]{1,0:T(8,128)} fusion(f32[512,128]{0,1:T(8,128)} %reduce-scatter.3.cloned.1.call-done, f32[512,512]{1,0:T(8,128)S(1)} %get-tuple-element.99), kind=kOutput, calls=%fused_computation.31 | convolution fusion | flops 402653184 | bytes 1572864 | tf_op jit(solution)/shard_map/dot_general | solution.py:59
  46.3 0.0 all-reduce.2.cloned.1.call-start
  46.4 0.7 constant_dynamic-slice_fusion.2
  47.1 21.8 %reduce-scatter.5.cloned.1.call-done = f32[128,128]{1,0:T(8,128)} async-done(((f32[128,512]{1,0:T(8,128)}), f32[128,128]{1,0:T(8,128)}) %reduce-scatter.5.cloned.1.call-update) | async-done | bytes 65552 | tf_op jit(solution)/shard_map/reduce_scatter | solution.py:66
  68.9 3.1 %fusion.2 = f32[128,32,32]{0,2,1:T(8,128)S(1)} fusion(f32[32,128]{1,0:T(8,128)S(1)} %constant_dynamic-slice_fusion.2, f32[128,128]{1,0:T(8,128)} %reduce-scatter.5.cloned.1.call-done, f32[32,512]{1,0:T(8,128)S(1)} %copy-done, s32[]{:T(128)S(6)} %select_n.26), kind=kOutput, calls=%fused_computation.6 | convolution fusion | flops 201850880 | bytes 622596 | tf_op jit(solution)/shard_map/dot_general | solution.py:18
  72.0 0.6 reshape.13
  72.6 1.1 copy.7
  73.8 0.0 all-reduce.2.cloned.1.call-update
  73.8 130.2 %all-reduce.2.cloned.1.call-done = f32[2,64,32,32]{1,3,2,0:T(8,128)} async-done(((f32[2,64,32,32]{1,3,2,0:T(8,128)}), f32[2,64,32,32]{1,3,2,0:T(8,128)}) %all-reduce.2.cloned.1.call-update) | async-done | bytes 524304 | tf_op jit(solution)/shard_map/psum | solution.py:72
  204.0 2.3 %copy.15 = f32[2,64,32,32]{1,3,2,0:T(8,128)} copy(f32[2,64,32,32]{1,3,2,0:T(8,128)} %all-reduce.2.cloned.1.call-done) | data formatting | bytes 1048576
  (22 shorter events, 0.1 us)
Async XLA Ops:
  6.5 62.4 %copy-start = (f32[32,512]{1,0:T(8,128)S(1)}, f32[32,512]{1,0:T(8,128)}, u32[]{:S(2)}) copy-start(f32[32,512]{1,0:T(8,128)} %param.13) | copy-start | bytes 196612
  6.5 37.4 %reduce-scatter.3.cloned.1.call-start = ((), (), s32[]{:S(2)}) async-start(), calls=%async_computation.2 | async-start | bytes 1310720 | tf_op jit(solution)/shard_map/reduce_scatter | solution.py:46
  16.2 52.7 %reduce-scatter.5.cloned.1.call-start = ((), (), s32[]{:S(2)}) async-start(), calls=%async_computation.3 | async-start | bytes 327680 | tf_op jit(solution)/shard_map/reduce_scatter | solution.py:66
  46.3 157.7 %all-reduce.2.cloned.1.call-start = ((), (), s32[]{:S(2)}) async-start(), calls=%async_computation.4 | async-start | bytes 2097152 | tf_op jit(solution)/shard_map/psum | solution.py:72
Sparse Core Ops, SparseCore 0:
  16.3 27.5 reduce-scatter.2
  46.5 22.3 reduce-scatter.4
  74.1 129.8 all-reduce.1
where the time goes:
time: 216 us; the launch traced here: 213 us
  waiting for transfers between devices  152 us (70%)
  local copies, waits for them, and re-layouts  27.9 us (13%)
  matrix products  13.3 us (6%)
  between operations  13.1 us (6%)
  other arithmetic  5.54 us (3%)
    psum x1, waiting for transfers between devices, body(): summed = lax.psum(local_grams, ('tm', 'panel'))  130 us
    reduce_scatter x1, waiting for transfers between devices, body(): lax.psum_scatter(partial_spectra, 'tm', scatter_dimension=1, tiled=True)  21.8 us
    dynamic_slice x16, local copies, waits for them, and re-layouts, add_column(): weight_column = lax.dynamic_slice_in_dim(spline_weights, column, 1, 1)[:, 0]  11.6 us
    dynamic_slice x16, local copies, waits for them, and re-layouts, add_column(): ids_column = lax.dynamic_slice_in_dim(stencil_ids, column, 1, 1)[:, 0]  11.6 us
    dot_general x1, matrix products, body(): lax.dot_general(pressure, local_table, (((0,), (1,)), ((), ())), precisio...  7.85 us
  transfers between devices with their start and end apart: 3, of which 3 were waited for; matrix products, arithmetic and copies ran while one was open for 13% of the time, Pallas kernels for 0%

commit v1 on v0

--- a/solution.py
+++ b/solution.py
@@ -69,7 +69,8 @@
     forces_own = lax.dynamic_slice_in_dim(mode_forces, begin, owned_width, 1)
     washes_own = lax.dynamic_slice_in_dim(mode_washes, begin, owned_width, 1)
     local_grams = modal_matrices(owned, forces_own, washes_own)
-    summed = lax.psum(local_grams, ("tm", "panel"))
+    shards = lax.all_gather(local_grams, ("tm", "panel"))
+    summed = jnp.sum(shards, axis=0)
     modes = mode_forces.shape[0]
     return summed.reshape(2, -1, modes, modes)
 

time: 216 us -> 248 us (1.15)
  local copies, waits for them, and re-layouts: 27.9 us -> 39.7 us
  waiting for transfers between devices: 152 us -> 162 us
  other arithmetic: 5.54 us -> 14.2 us
    all_gather x0 -> x1, waiting for transfers between devices: none -> 140 us  [body(): shards = lax.all_gather(local_grams, ('tm', 'panel'))]
    psum x1 -> x0, waiting for transfers between devices: 130 us -> none  [body(): summed = lax.psum(local_grams, ('tm', 'panel'))]
    unnamed x3, local copies, waits for them, and re-layouts: 2.27 us -> 14.1 us
    reduce_sum x0 -> x1, other arithmetic: none -> 8.64 us  [body(): summed = jnp.sum(shards, axis=0)]
  transfers between devices with their start and end apart: 3 -> 3, of which waited for: 3 -> 3; matrix products, arithmetic and copies ran while one was open for 13% -> 11% of each run, Pallas kernels for 0% -> 0%
where the time goes in v1:
time: 248 us; the launch traced here: 244 us
  waiting for transfers between devices  162 us (65%)
  local copies, waits for them, and re-layouts  39.7 us (16%)
  other arithmetic  14.2 us (6%)
  matrix products  14.1 us (6%)
  between operations  13.1 us (5%)
    all_gather x1, waiting for transfers between devices, body(): shards = lax.all_gather(local_grams, ('tm', 'panel'))  140 us
    reduce_scatter x1, waiting for transfers between devices, body(): lax.psum_scatter(partial_spectra, 'tm', scatter_dimension=1, tiled=True)  21.8 us
    unnamed x3, local copies, waits for them, and re-layouts  14.1 us
    dynamic_slice x16, local copies, waits for them, and re-layouts, add_column(): weight_column = lax.dynamic_slice_in_dim(spline_weights, column, 1, 1)[:, 0]  11.6 us
    dynamic_slice x16, local copies, waits for them, and re-layouts, add_column(): ids_column = lax.dynamic_slice_in_dim(stencil_ids, column, 1, 1)[:, 0]  11.6 us
    reduce_sum x1, other arithmetic, body(): summed = jnp.sum(shards, axis=0)  8.64 us
    dot_general x1, matrix products, body(): lax.dot_general(pressure, local_table, (((0,), (1,)), ((), ())), precisio...  7.85 us
  transfers between devices with their start and end apart: 3, of which 3 were waited for; matrix products, arithmetic and copies ran while one was open for 11% of the time, Pallas kernels for 0%

profile of v1, /device:TPU:0, one launch (start us, length us, event | category | flops | bytes accessed | tf_op | source)
XLA Modules:
  0.0 244.1 jit_solution(11639418356745347016)
XLA Ops:
  6.5 1.8 fusion.12
  8.3 7.8 %convolution_bitcast_fusion = f32[2048,128]{0,1:T(8,128)} fusion(f32[1024,2048]{1,0:T(8,128)} %param.8, f32[64,1024]{1,0:T(8,128)S(1)} %get-tuple-element.132, f32[64,1024]{1,0:T(8,128)S(1)} %get-tuple-element.131), kind=kOutput, calls=%fused_computation.5 | convolution fusion | flops 3221487616 | bytes 9961472 | tf_op jit(solution)/shard_map/dot_general | solution.py:47
  16.2 0.0 reduce-scatter.3.cloned.1.call-update
  16.2 0.0 reduce-scatter.5.cloned.1.call-start
  16.3 27.4 %while.14 = (s32[]{:T(128)}, f32[512,512]{1,0:T(8,128)S(1)}, s32[512,16]{0,1:T(8,128)}, f32[512,16]{0,1:T(8,128)}, s32[]{:T(128)}, /*index=5*/s32[]{:T(128)}, s32[]{:T(128)}) while((s32[]{:T(128)}, f32[512,512]{1,0:T(8,128)S(1)}, s32[512,16]{0,1:T(8,128)}, f32[512,16]{0,1:T(8,128)}, s32[]{:T(128)}, /*index=5*/s32[]{:T(128)}, ...), condition=%wide.region_2.3_spmd.clone, body=%wide.region_1.2_spmd.clone.sunk | while | flops 1049091 | bytes 2113643 | solution.py:36
  16.3 0.7 constant_dynamic-slice_fusion.5
  17.0 0.7 constant_dynamic-slice_fusion.6
  17.7 0.2 select_add_fusion.2
  18.0 0.7 constant_dynamic-slice_fusion.5
  18.7 0.7 constant_dynamic-slice_fusion.6
  19.4 0.2 select_add_fusion.2
  19.7 0.7 constant_dynamic-slice_fusion.5
  20.4 0.7 constant_dynamic-slice_fusion.6
  21.2 0.2 select_add_fusion.2
  21.4 0.7 constant_dynamic-slice_fusion.5
  22.1 0.7 constant_dynamic-slice_fusion.6
  22.9 0.2 select_add_fusion.2
  23.1 0.7 constant_dynamic-slice_fusion.5
  23.8 0.7 constant_dynamic-slice_fusion.6
  24.6 0.2 select_add_fusion.2
  24.8 0.7 constant_dynamic-slice_fusion.5
  25.6 0.7 constant_dynamic-slice_fusion.6
  26.3 0.2 select_add_fusion.2
  26.5 0.7 constant_dynamic-slice_fusion.5
  27.3 0.7 constant_dynamic-slice_fusion.6
  28.0 0.2 select_add_fusion.2
  28.3 0.7 constant_dynamic-slice_fusion.5
  29.0 0.7 constant_dynamic-slice_fusion.6
  29.7 0.2 select_add_fusion.2
  30.0 0.7 constant_dynamic-slice_fusion.5
  30.7 0.7 constant_dynamic-slice_fusion.6
  31.4 0.2 select_add_fusion.2
  31.7 0.7 constant_dynamic-slice_fusion.5
  32.4 0.7 constant_dynamic-slice_fusion.6
  33.1 0.2 select_add_fusion.2
  33.4 0.7 constant_dynamic-slice_fusion.5
  34.1 0.7 constant_dynamic-slice_fusion.6
  34.8 0.2 select_add_fusion.2
  35.1 0.7 constant_dynamic-slice_fusion.5
  35.8 0.7 constant_dynamic-slice_fusion.6
  36.6 0.2 select_add_fusion.2
  36.8 0.7 constant_dynamic-slice_fusion.5
  37.5 0.7 constant_dynamic-slice_fusion.6
  38.3 0.2 select_add_fusion.2
  38.5 0.7 constant_dynamic-slice_fusion.5
  39.2 0.7 constant_dynamic-slice_fusion.6
  40.0 0.2 select_add_fusion.2
  40.2 0.7 constant_dynamic-slice_fusion.5
  41.0 0.7 constant_dynamic-slice_fusion.6
  41.7 0.2 select_add_fusion.2
  41.9 0.7 constant_dynamic-slice_fusion.5
  42.7 0.7 constant_dynamic-slice_fusion.6
  43.4 0.2 select_add_fusion.2
  43.6 0.3 reduce-scatter.3.cloned.1.call-done
  43.9 2.4 fusion.18
  46.3 0.0 all-gather.3.cloned.1.call-start
  46.4 0.7 constant_dynamic-slice_fusion.2
  47.1 21.8 %reduce-scatter.5.cloned.1.call-done = f32[128,128]{1,0:T(8,128)} async-done(((f32[128,512]{1,0:T(8,128)}), f32[128,128]{1,0:T(8,128)}) %reduce-scatter.5.cloned.1.call-update) | async-done | bytes 65552 | tf_op jit(solution)/shard_map/reduce_scatter | solution.py:66
  68.9 3.9 %fusion.2 = f32[128,32,32]{0,2,1:T(8,128)} fusion(f32[32,128]{1,0:T(8,128)S(1)} %constant_dynamic-slice_fusion.2, f32[128,128]{1,0:T(8,128)} %reduce-scatter.5.cloned.1.call-done, f32[32,512]{1,0:T(8,128)S(1)} %copy-done, s32[]{:T(128)S(6)} %select_n.26), kind=kOutput, calls=%fused_computation.6 | convolution fusion | flops 201850880 | bytes 622596 | tf_op jit(solution)/shard_map/dot_general | solution.py:18
  72.8 140.3 %all-gather.3.cloned.1.call-done = f32[4096,32,32]{0,2,1:T(8,128)} async-done(((f32[128,32,32]{0,2,1:T(8,128)}), f32[4096,32,32]{0,2,1:T(8,128)}) %all-gather.3.cloned.1.call-update) | async-done | bytes 16777232 | tf_op jit(solution)/shard_map/all_gather | solution.py:72
  213.1 14.1 %copy.8 = f32[128,8,32,128]{3,2,1,0:T(8,128)} copy(f32[128,8,32,128]{3,1,2,0:T(8,128)} %bitcast.23) | data formatting | bytes 33554432
  227.2 8.6 %reduce_sum.9 = f32[128,32,32]{0,2,1:T(8,128)S(1)} reduce(f32[32,128,32,32]{1,0,3,2:T(8,128)} %bitcast.22, f32[]{:T(128)} %constant.59.clone.1), dimensions={0}, to_apply=%region_4.5 | reduce | flops 4063232 | bytes 17301508 | tf_op jit(solution)/shard_map/reduce_sum | solution.py:73
  235.8 0.6 reshape.13
  236.5 1.1 copy.7
  (23 shorter events, 0.1 us)
Async XLA Ops:
  6.5 62.4 %copy-start = (f32[32,512]{1,0:T(8,128)S(1)}, f32[32,512]{1,0:T(8,128)}, u32[]{:S(2)}) copy-start(f32[32,512]{1,0:T(8,128)} %param.13) | copy-start | bytes 196612
  6.5 37.4 %reduce-scatter.3.cloned.1.call-start = ((), (), s32[]{:S(2)}) async-start(), calls=%async_computation.2 | async-start | bytes 1310720 | tf_op jit(solution)/shard_map/reduce_scatter | solution.py:46
  16.2 52.7 %reduce-scatter.5.cloned.1.call-start = ((), (), s32[]{:S(2)}) async-start(), calls=%async_computation.3 | async-start | bytes 327680 | tf_op jit(solution)/shard_map/reduce_scatter | solution.py:66
  46.3 166.8 %all-gather.3.cloned.1.call-start = ((), (), s32[]{:S(2)}) async-start(), calls=%async_computation.4 | async-start | bytes 17301504 | tf_op jit(solution)/shard_map/all_gather | solution.py:72
Sparse Core Ops, SparseCore 0:
  16.3 27.5 reduce-scatter.2
  46.5 22.3 reduce-scatter.4
  73.0 140.0 all-gather.2

commit v2 on v0

--- a/solution.py
+++ b/solution.py
@@ -69,7 +69,9 @@
     forces_own = lax.dynamic_slice_in_dim(mode_forces, begin, owned_width, 1)
     washes_own = lax.dynamic_slice_in_dim(mode_washes, begin, owned_width, 1)
     local_grams = modal_matrices(owned, forces_own, washes_own)
-    summed = lax.psum(local_grams, ("tm", "panel"))
+    summed = local_grams
+    for i0 in ("panel", "tm"):
+        summed = jax.lax.psum(summed, i0)
     modes = mode_forces.shape[0]
     return summed.reshape(2, -1, modes, modes)
 

time: 216 us -> 196 us (0.907)
  waiting for transfers between devices: 152 us -> 130 us
    psum x1 -> x2, waiting for transfers between devices: 130 us -> 108 us  [body(): summed = jax.lax.psum(summed, i0)]
  transfers between devices with their start and end apart: 3 -> 4, of which waited for: 3 -> 4; matrix products, arithmetic and copies ran while one was open for 13% -> 14% of each run, Pallas kernels for 0% -> 0%
where the time goes in v2:
time: 196 us; the launch traced here: 192 us
  waiting for transfers between devices  130 us (66%)
  local copies, waits for them, and re-layouts  28.9 us (15%)
  matrix products  14.1 us (7%)
  between operations  13.2 us (7%)
  other arithmetic  5.54 us (3%)
    psum x2, waiting for transfers between devices, body(): summed = jax.lax.psum(summed, i0)  108 us
    reduce_scatter x1, waiting for transfers between devices, body(): lax.psum_scatter(partial_spectra, 'tm', scatter_dimension=1, tiled=True)  21.8 us
    dynamic_slice x16, local copies, waits for them, and re-layouts, add_column(): weight_column = lax.dynamic_slice_in_dim(spline_weights, column, 1, 1)[:, 0]  11.6 us
    dynamic_slice x16, local copies, waits for them, and re-layouts, add_column(): ids_column = lax.dynamic_slice_in_dim(stencil_ids, column, 1, 1)[:, 0]  11.6 us
    dot_general x1, matrix products, body(): lax.dot_general(pressure, local_table, (((0,), (1,)), ((), ())), precisio...  7.85 us
  transfers between devices with their start and end apart: 4, of which 4 were waited for; matrix products, arithmetic and copies ran while one was open for 14% of the time, Pallas kernels for 0%

profile of v2, /device:TPU:0, one launch (start us, length us, event | category | flops | bytes accessed | tf_op | source)
XLA Modules:
  0.0 192.5 jit_solution(14717601810612268748)
XLA Ops:
  6.5 1.8 fusion.12
  8.3 7.8 %convolution_bitcast_fusion = f32[2048,128]{0,1:T(8,128)} fusion(f32[1024,2048]{1,0:T(8,128)} %param.8, f32[64,1024]{1,0:T(8,128)S(1)} %get-tuple-element.132, f32[64,1024]{1,0:T(8,128)S(1)} %get-tuple-element.131), kind=kOutput, calls=%fused_computation.5 | convolution fusion | flops 3221487616 | bytes 9961472 | tf_op jit(solution)/shard_map/dot_general | solution.py:47
  16.2 0.0 reduce-scatter.5.cloned.1.call-start
  16.3 27.4 %while.14 = (s32[]{:T(128)}, f32[512,512]{1,0:T(8,128)S(1)}, s32[512,16]{0,1:T(8,128)}, f32[512,16]{0,1:T(8,128)}, s32[]{:T(128)}, /*index=5*/s32[]{:T(128)}, s32[]{:T(128)}) while((s32[]{:T(128)}, f32[512,512]{1,0:T(8,128)S(1)}, s32[512,16]{0,1:T(8,128)}, f32[512,16]{0,1:T(8,128)}, s32[]{:T(128)}, /*index=5*/s32[]{:T(128)}, ...), condition=%wide.region_2.3_spmd.clone, body=%wide.region_1.2_spmd.clone.sunk | while | flops 1049091 | bytes 2113643 | solution.py:36
  16.3 0.7 constant_dynamic-slice_fusion.5
  17.0 0.7 constant_dynamic-slice_fusion.6
  17.7 0.2 select_add_fusion.2
  18.0 0.7 constant_dynamic-slice_fusion.5
  18.7 0.7 constant_dynamic-slice_fusion.6
  19.4 0.2 select_add_fusion.2
  19.7 0.7 constant_dynamic-slice_fusion.5
  20.4 0.7 constant_dynamic-slice_fusion.6
  21.2 0.2 select_add_fusion.2
  21.4 0.7 constant_dynamic-slice_fusion.5
  22.1 0.7 constant_dynamic-slice_fusion.6
  22.9 0.2 select_add_fusion.2
  23.1 0.7 constant_dynamic-slice_fusion.5
  23.8 0.7 constant_dynamic-slice_fusion.6
  24.6 0.2 select_add_fusion.2
  24.8 0.7 constant_dynamic-slice_fusion.5
  25.6 0.7 constant_dynamic-slice_fusion.6
  26.3 0.2 select_add_fusion.2
  26.5 0.7 constant_dynamic-slice_fusion.5
  27.3 0.7 constant_dynamic-slice_fusion.6
  28.0 0.2 select_add_fusion.2
  28.3 0.7 constant_dynamic-slice_fusion.5
  29.0 0.7 constant_dynamic-slice_fusion.6
  29.7 0.2 select_add_fusion.2
  30.0 0.7 constant_dynamic-slice_fusion.5
  30.7 0.7 constant_dynamic-slice_fusion.6
  31.4 0.2 select_add_fusion.2
  31.7 0.7 constant_dynamic-slice_fusion.5
  32.4 0.7 constant_dynamic-slice_fusion.6
  33.1 0.2 select_add_fusion.2
  33.4 0.7 constant_dynamic-slice_fusion.5
  34.1 0.7 constant_dynamic-slice_fusion.6
  34.8 0.2 select_add_fusion.2
  35.1 0.7 constant_dynamic-slice_fusion.5
  35.8 0.7 constant_dynamic-slice_fusion.6
  36.6 0.2 select_add_fusion.2
  36.8 0.7 constant_dynamic-slice_fusion.5
  37.5 0.7 constant_dynamic-slice_fusion.6
  38.3 0.2 select_add_fusion.2
  38.5 0.7 constant_dynamic-slice_fusion.5
  39.2 0.7 constant_dynamic-slice_fusion.6
  40.0 0.2 select_add_fusion.2
  40.2 0.7 constant_dynamic-slice_fusion.5
  41.0 0.7 constant_dynamic-slice_fusion.6
  41.7 0.2 select_add_fusion.2
  41.9 0.7 constant_dynamic-slice_fusion.5
  42.7 0.7 constant_dynamic-slice_fusion.6
  43.4 0.2 select_add_fusion.2
  43.6 0.3 reduce-scatter.3.cloned.1.call-done
  43.9 2.4 %fusion.18 = f32[128,512]{1,0:T(8,128)} fusion(f32[512,128]{0,1:T(8,128)} %reduce-scatter.3.cloned.1.call-done, f32[512,512]{1,0:T(8,128)S(1)} %get-tuple-element.99), kind=kOutput, calls=%fused_computation.31 | convolution fusion | flops 402653184 | bytes 1572864 | tf_op jit(solution)/shard_map/dot_general | solution.py:59
  46.3 0.0 all-reduce.3.cloned.1.call-start
  46.4 0.7 constant_dynamic-slice_fusion.2
  47.1 21.8 %reduce-scatter.5.cloned.1.call-done = f32[128,128]{1,0:T(8,128)} async-done(((f32[128,512]{1,0:T(8,128)}), f32[128,128]{1,0:T(8,128)}) %reduce-scatter.5.cloned.1.call-update) | async-done | bytes 65552 | tf_op jit(solution)/shard_map/reduce_scatter | solution.py:66
  68.9 3.9 %fusion.2 = f32[128,32,32]{0,2,1:T(8,128)} fusion(f32[32,128]{1,0:T(8,128)S(1)} %constant_dynamic-slice_fusion.2, f32[128,128]{1,0:T(8,128)} %reduce-scatter.5.cloned.1.call-done, f32[32,512]{1,0:T(8,128)S(1)} %copy-done, s32[]{:T(128)S(6)} %select_n.26), kind=kOutput, calls=%fused_computation.6 | convolution fusion | flops 201850880 | bytes 622596 | tf_op jit(solution)/shard_map/dot_general | solution.py:18
  72.8 0.0 all-reduce.5.cloned.1.call-start
  72.9 72.5 %all-reduce.3.cloned.1.call-done = f32[128,32,32]{0,2,1:T(8,128)} async-done(((f32[128,32,32]{0,2,1:T(8,128)}), f32[128,32,32]{0,2,1:T(8,128)}) %all-reduce.3.cloned.1.call-update) | async-done | bytes 524304 | tf_op jit(solution)/shard_map/psum | solution.py:74
  145.4 1.6 reshape.13
  147.0 1.1 copy.7
  148.2 35.5 %all-reduce.5.cloned.1.call-done = f32[2,64,32,32]{1,3,2,0:T(8,128)} async-done(((f32[2,64,32,32]{1,3,2,0:T(8,128)}), f32[2,64,32,32]{1,3,2,0:T(8,128)}) %all-reduce.5.cloned.1.call-update) | async-done | bytes 524304 | tf_op jit(solution)/shard_map/psum | solution.py:74
  183.7 2.3 %copy.16 = f32[2,64,32,32]{1,3,2,0:T(8,128)} copy(f32[2,64,32,32]{1,3,2,0:T(8,128)} %all-reduce.5.cloned.1.call-done) | data formatting | bytes 1048576
  (25 shorter events, 0.1 us)
Async XLA Ops:
  6.5 62.4 %copy-start = (f32[32,512]{1,0:T(8,128)S(1)}, f32[32,512]{1,0:T(8,128)}, u32[]{:S(2)}) copy-start(f32[32,512]{1,0:T(8,128)} %param.13) | copy-start | bytes 196612
  6.5 37.4 %reduce-scatter.3.cloned.1.call-start = ((), (), s32[]{:S(2)}) async-start(), calls=%async_computation.2 | async-start | bytes 1310720 | tf_op jit(solution)/shard_map/reduce_scatter | solution.py:46
  16.2 52.7 %reduce-scatter.5.cloned.1.call-start = ((), (), s32[]{:S(2)}) async-start(), calls=%async_computation.3 | async-start | bytes 327680 | tf_op jit(solution)/shard_map/reduce_scatter | solution.py:66
  46.3 99.1 %all-reduce.3.cloned.1.call-start = ((), (), s32[]{:S(2)}) async-start(), calls=%async_computation.4 | async-start | bytes 1048576 | tf_op jit(solution)/shard_map/psum | solution.py:74
  72.8 110.8 %all-reduce.5.cloned.1.call-start = ((), (), s32[]{:S(2)}) async-start(), calls=%async_computation.5 | async-start | bytes 2097152 | tf_op jit(solution)/shard_map/psum | solution.py:74
Sparse Core Ops, SparseCore 0:
  16.3 27.5 reduce-scatter.2
  46.5 22.3 reduce-scatter.4
  73.0 72.3 all-reduce.2
  148.3 35.3 all-reduce.4
